TPU v7x, 768 devices: a whole 4x8x12 slice. The times are simulated.
768 devices in a mesh: row: 96 (over x, z, core), col: 8 (over y).
Axes of the slice: x: 4, y: 8, z: 12, core: 2. Of those that a mesh axis runs over, the one named last changes fastest.
Arguments:
- features: float32 [49152, 128], P(('row', 'col')), may hold values from -6 to 6
- tile_coords: int32 [96, 8, 54, 2], P('row', 'col'), may hold values from 0 to 47, as said below
- tile_count: int32 [96, 8], P('row', 'col'), may hold values from 13 to 54, as said below
- tile_values: bfloat16 [96, 8, 54, 128, 128], P('row', 'col'), may hold values from -0.078125 to 0.078125
- w_first: float32 [128, 128], replicated, may hold values from -0.5 to 0.5
- bias_first: float32 [128], replicated, may hold values from -3 to 3
- w_second: float32 [128, 128], replicated, may hold values from -0.5 to 0.5
- bias_second: float32 [128], replicated, may hold values from -3 to 3
Outputs:
- node_out: float32 [49152, 128], P(('row', 'col'))
Inputs may be any that keep to these rules, and one draw needn't show every extreme that they name: `tile_coords`: each slot holds a tile row below 4 and a tile column below 48; the 54 pairs of one device are distinct. The first tile_count slots of a device are in use; some device uses all 54.
All inputs are finite; a program needn't handle non-finite values.
Results may differ from a plain program's by a relative error of at most 0.0034.
Values may be sent and summed in bfloat16 or wider, within the bound.
A program may use at most 32 MiB of HBM per device.

v0:
```python
import jax
import jax.numpy as jnp
from jax import lax
from jax.sharding import PartitionSpec as P


def aggregate(node_rows, weight, coords, used_count, values):
    tile_size = values.shape[1]
    slot_total = values.shape[0]
    out_width = weight.shape[1]
    own_rows = node_rows.shape[0]
    column = lax.all_gather(node_rows, "row", axis=0, tiled=True)
    mixed = jnp.dot(
        column, weight, precision=lax.Precision.HIGHEST, preferred_element_type=jnp.float32
    ).astype(jnp.bfloat16)
    col_tiles = mixed.reshape(-1, tile_size, out_width)
    picked = jnp.take(col_tiles, coords[:, 1], axis=0)
    products = jnp.einsum("kab,kbf->kaf", values, picked, preferred_element_type=jnp.float32)
    row_tiles = lax.axis_size("col") * own_rows // tile_size
    live = jnp.arange(slot_total, dtype=jnp.int32) < used_count
    chosen = (
        (coords[:, 0][None, :] == jnp.arange(row_tiles, dtype=jnp.int32)[:, None]) & live[None, :]
    ).astype(jnp.float32)
    summed = jnp.einsum("rk,kaf->raf", chosen, products, precision=lax.Precision.HIGHEST)
    summed = summed.reshape(row_tiles * tile_size, out_width)
    whole = lax.psum(summed, "col")
    return lax.dynamic_slice_in_dim(whole, lax.axis_index("col") * own_rows, own_rows, 0)


def on_device(
    features, tile_coords, tile_count, tile_values, w_first, bias_first, w_second, bias_second
):
    coords = tile_coords[0, 0]
    used_count = tile_count[0, 0]
    values = tile_values[0, 0]
    agg_first = aggregate(features, w_first, coords, used_count, values)
    h_first = jnp.maximum(agg_first + bias_first, 0.0)
    agg_second = aggregate(h_first, w_second, coords, used_count, values)
    return agg_second + bias_second


def solution(mesh):
    return jax.shard_map(
        on_device,
        mesh=mesh,
        in_specs=(
            P(("row", "col"), None),
            P("row", "col", None, None),
            P("row", "col"),
            P("row", "col", None, None, None),
            P(),
            P(),
            P(),
            P(),
        ),
        out_specs=P(("row", "col"), None),
        check_vma=False,
    )
```

profile of v0, /device:TPU:1, one launch (start us, length us, event | category | flops | bytes accessed | tf_op | source)
XLA Modules:
  0.0 457.9 jit_solution(12590191411744939445)
XLA Ops:
  6.5 0.0 copy-start
  6.5 0.0 all-gather.3.cloned.1.call-start
  6.5 0.7 all-gather.3.cloned.1.call-update
  7.3 0.0 all-reduce.3.cloned.1.call-start
  8.0 0.7 compare_and_fusion
  8.7 0.7 slice_bitcast_fusion
  9.3 126.5 %all-gather.3.cloned.1.call-done = f32[6144,128]{1,0:T(8,128)} async-done(((f32[64,128]{1,0:T(8,128)}), f32[6144,128]{1,0:T(8,128)}) %all-gather.3.cloned.1.call-update) | async-done | bytes 3145744 | tf_op jit(solution)/shard_map/all_gather | solution.py:12
  135.9 4.2 convolution_convert_fusion.1
  140.1 2.0 gather_fusion
  142.1 0.0 copy-done
  142.1 4.8 %fusion.6 = f32[54,128,128]{2,1,0:T(8,128)} fusion(bf16[1,1,54,128,128]{4,3,2,1,0:T(8,128)(2,1)S(1)} %copy-done, bf16[54,128,128]{2,1,0:T(8,128)(2,1)} %gather_fusion, pred[54]{0:T(512)(128)(4,1)S(1)} %get-tuple-element.6), kind=kOutput, calls=%fused_computation.10 | convolution fusion | flops 227377152 | bytes 7077942 | tf_op jit(solution)/shard_map/kab,kbf->kaf/dot_general | solution.py:18
  146.9 4.5 copy.11
  151.4 3.4 fusion.2
  154.8 0.7 copy.9
  155.5 0.0 all-reduce.3.cloned.1.call-update
  155.5 0.0 all-gather.5.cloned.1.call-start
  155.6 75.2 %all-reduce.3.cloned.1.call-done = f32[512,128]{1,0:T(8,128)} async-done(((f32[512,128]{1,0:T(8,128)}), f32[512,128]{1,0:T(8,128)}) %all-reduce.3.cloned.1.call-update) | async-done | bytes 262160 | tf_op jit(solution)/shard_map/psum | solution.py:26
  230.7 0.0 copy-done.2
  230.7 1.4 add_maximum_fusion
  232.1 0.0 all-gather.5.cloned.1.call-update
  232.1 0.0 all-reduce.5.cloned.1.call-start
  232.2 123.0 %all-gather.5.cloned.1.call-done = f32[6144,128]{1,0:T(8,128)} async-done(((f32[64,128]{1,0:T(8,128)}), f32[6144,128]{1,0:T(8,128)}) %all-gather.5.cloned.1.call-update) | async-done | bytes 3145744 | tf_op jit(solution)/shard_map/all_gather | solution.py:12
  355.2 0.0 copy-done.1
  355.2 4.2 convolution_convert_fusion
  359.4 2.0 gather_fusion.1
  361.4 4.8 %fusion.4 = f32[54,128,128]{2,1,0:T(8,128)} fusion(bf16[1,1,54,128,128]{4,3,2,1,0:T(8,128)(2,1)S(1)} %copy-done, bf16[54,128,128]{2,1,0:T(8,128)(2,1)} %gather_fusion.1, pred[54]{0:T(512)(128)(4,1)S(1)} %get-tuple-element.6), kind=kOutput, calls=%fused_computation.8 | convolution fusion | flops 227377152 | bytes 7077942 | tf_op jit(solution)/shard_map/kab,kbf->kaf/dot_general | solution.py:18
  366.2 4.5 copy.12
  370.7 3.4 fusion
  374.1 0.7 copy.10
  374.8 0.0 all-reduce.5.cloned.1.call-update
  374.8 75.2 %all-reduce.5.cloned.1.call-done = f32[512,128]{1,0:T(8,128)} async-done(((f32[512,128]{1,0:T(8,128)}), f32[512,128]{1,0:T(8,128)}) %all-reduce.5.cloned.1.call-update) | async-done | bytes 262160 | tf_op jit(solution)/shard_map/psum | solution.py:26
  450.0 1.4 dynamic-slice_add_fusion
  (6 shorter events, 0.0 us)
Async XLA Ops:
  6.5 135.6 %copy-start = (bf16[1,1,54,128,128]{4,3,2,1,0:T(8,128)(2,1)S(1)}, bf16[1,1,54,128,128]{4,3,2,1,0:T(8,128)(2,1)}, u32[]{:S(2)}) copy-start(bf16[1,1,54,128,128]{4,3,2,1,0:T(8,128)(2,1)} %param.13) | copy-start | bytes 5308420
  6.5 129.4 %all-gather.3.cloned.1.call-start = ((), (), s32[]{:S(2)}) async-start(), calls=%async_computation | async-start | bytes 3178496 | tf_op jit(solution)/shard_map/all_gather | solution.py:12
  7.3 223.5 %all-reduce.3.cloned.1.call-start = ((), (), s32[]{:S(2)}) async-start(), calls=%async_computation.1 | async-start | bytes 524288 | tf_op jit(solution)/shard_map/psum | solution.py:26
  151.4 79.3 %copy-start.2 = (f32[128]{0:T(128)S(1)}, f32[128]{0:T(128)}, u32[]{:S(2)}) copy-start(f32[128]{0:T(128)} %param.15) | copy-start | bytes 1540
  151.4 203.8 %copy-start.1 = (f32[128,128]{1,0:T(8,128)S(1)}, f32[128,128]{1,0:T(8,128)}, u32[]{:S(2)}) copy-start(f32[128,128]{1,0:T(8,128)} %param.16) | copy-start | bytes 196612
  155.5 199.7 %all-gather.5.cloned.1.call-start = ((), (), s32[]{:S(2)}) async-start(), calls=%async_computation.2 | async-start | bytes 3178496 | tf_op jit(solution)/shard_map/all_gather | solution.py:12
  232.1 217.9 %all-reduce.5.cloned.1.call-start = ((), (), s32[]{:S(2)}) async-start(), calls=%async_computation.3 | async-start | bytes 524288 | tf_op jit(solution)/shard_map/psum | solution.py:26
  370.7 79.3 %copy-start.3 = (f32[128]{0:T(128)S(1)}, f32[128]{0:T(128)}, u32[]{:S(2)}) copy-start(f32[128]{0:T(128)} %param.17) | copy-start | bytes 1540
Sparse Core Ops, SparseCore 0:
  11.0 124.8 all-gather.2
  155.6 75.0 all-reduce.2
  235.0 120.1 all-gather.4
  374.9 75.0 all-reduce.4
where the time goes:
time: 462 us; the launch traced here: 458 us
  waiting for transfers between devices  401 us (87%)
  matrix products  24.7 us (5%)
  local copies, waits for them, and re-layouts  15.1 us (3%)
  between operations  13.8 us (3%)
    all_gather x2, waiting for transfers between devices, aggregate(): column = lax.all_gather(node_rows, 'row', axis=0, tiled=True)  250 us
    psum x2, waiting for transfers between devices, aggregate(): whole = lax.psum(summed, 'col')  150 us
    dot_general x2, matrix products, aggregate(): jnp.einsum('kab,kbf->kaf', values, picked, preferred_element_type=jnp.flo...  9.59 us
  transfers between devices with their start and end apart: 4, of which 4 were waited for; matrix products, arithmetic and copies ran while one was open for 0% of the time, Pallas kernels for 0%

commit v1 on v0

v1 whole, which is shorter than its diff:
```python
import functools

import jax
import jax.numpy as jnp
from jax import lax
from jax.experimental import pallas as pl
from jax.experimental.pallas import tpu as pltpu
from jax.sharding import PartitionSpec as P

MESH = pl.DeviceIdType.MESH
NX, NZ, NY = 4, 12, 8
TILE, RT, SLOTS = 128, 4, 54
FAR_Z = (6, 5, -5, 4, -4, 3, -3, 2, -2, 1, -1)
FAR_X = (2, 1, -1)
FAR_Y = (4, 3, -3, 2, -2, 1, -1)


def kernel(
    slot_ref, feat_ref, tiles_hbm, w1_ref, b1_ref, w2_ref, b2_ref, out_ref,
    tiles, half, zb, acc, part1, part2, back2, tile_sem,
    half_send, half_recv, z_send, z_recv, x_send, x_recv, c_send, c_recv,
    r1_send, r1_recv, r2_send, r2_recv,
):
    row, col = lax.axis_index("row"), lax.axis_index("col")
    core = row % 2
    chip = row // 2
    z, x = chip % NZ, chip // NZ

    def at(dx, dz, c, dy=0):
        return (
            (((x + dx + NX) % NX) * NZ + (z + dz + NZ) % NZ) * 2 + c,
            (col + dy + NY) % NY,
        )

    def remote(src, dst, send, recv, to):
        return pltpu.make_async_remote_copy(
            src_ref=src, dst_ref=dst, send_sem=send, recv_sem=recv, device_id=to, device_id_type=MESH
        )

    def step_dz(t):
        return (((t + 1) // 2) * (2 * (t % 2) - 1) + NZ) % NZ

    load = pltpu.make_async_copy(tiles_hbm, tiles.at[pl.ds(0, SLOTS)], tile_sem)
    load.start()

    barrier = pltpu.get_barrier_semaphore()

    def signal(to):
        pl.semaphore_signal(barrier, inc=1, device_id=to, device_id_type=MESH)

    sibling = at(0, 0, 1 - core)
    signal(sibling)
    for d in FAR_Y:
        signal(at(0, 0, 0, d))

    @pl.when(core == 1)
    def _():
        for d in FAR_Z:
            signal(at(0, d, 1))
        for d in FAR_X:
            signal(at(d, 0, 1))
        for d in FAR_Y:
            signal(at(0, 0, 1, d))

    tiles[SLOTS] = jnp.zeros((TILE, TILE), jnp.bfloat16)
    mixed = jnp.dot(
        feat_ref[...], w1_ref[...], precision=lax.Precision.HIGHEST, preferred_element_type=jnp.float32
    ).astype(jnp.bfloat16)

    def half_copy():
        return remote(half, zb.at[0, 0, 0, pl.ds(0, 64)], half_send, half_recv, sibling)

    @pl.when(core == 0)
    def _():
        half[...] = mixed
        pl.semaphore_wait(barrier, 1 + 7 + 7)
        half_copy().start()

    @pl.when(core == 1)
    def _():
        zb[0, 0, 0, 64:128] = mixed
        pl.semaphore_wait(barrier, 1 + 7 + 11 + 3)
        half_copy().wait_recv()

    def z_copy(layer, i):
        d = FAR_Z[i]
        return remote(
            zb.at[layer, 0, 0], zb.at[layer, -d % NZ, 0],
            z_send.at[layer, i], z_recv.at[layer, -d % NZ], at(0, d, 1),
        )

    def x_copy(layer, dz, i):
        d = FAR_X[i]
        return remote(
            zb.at[layer, dz, 0], zb.at[layer, dz, -d % NX],
            x_send.at[layer, dz, i], x_recv.at[layer, dz], at(d, 0, 1),
        )

    def c_copy(layer, dz, first, size, i):
        block = zb.at[layer, dz, pl.ds(first, size)]
        return remote(block, block, c_send.at[layer, dz, i], c_recv.at[layer, dz], sibling)

    def multiply(layer, dz):
        za = (z + dz) % NZ
        places = [((x + dx) % NX) * NZ + za for dx in range(NX)]
        lhs = jnp.concatenate(
            [
                jnp.concatenate([tiles[slot_ref[r * NX * NZ + p]] for p in places], axis=1)
                for r in range(RT)
            ],
            axis=0,
        )
        rhs = zb[layer, dz].reshape(NX * TILE, TILE)
        acc[layer] += jnp.dot(lhs, rhs, preferred_element_type=jnp.float32).reshape(NY, 64, TILE)

    def gather_multiply(layer):
        acc[layer] = jnp.zeros((NY, 64, TILE), jnp.float32)

        @pl.when(core == 1)
        def _():
            for i in range(len(FAR_Z)):
                z_copy(layer, i).start()
            for i in range(len(FAR_X)):
                x_copy(layer, 0, i).start()
            c_copy(layer, 0, 0, 1, 0).start()

            @pl.loop(1, NZ)
            def _(t):
                dz = step_dz(t)
                remote(
                    zb.at[layer, dz, 0], zb.at[layer, dz, 0], z_send.at[layer, 0], z_recv.at[layer, dz], sibling
                ).wait_recv()
                for i in range(len(FAR_X)):
                    x_copy(layer, dz, i).start()
                c_copy(layer, dz, 0, 1, 0).start()

            if layer == 0:
                load.wait()

            @pl.loop(0, NZ)
            def _(t):
                dz = step_dz(t)
                rest = zb.at[layer, dz, pl.ds(1, NX - 1)]
                remote(rest, rest, c_send.at[layer, dz, 1], x_recv.at[layer, dz], sibling).wait_recv()
                c_copy(layer, dz, 1, NX - 1, 1).start()
                multiply(layer, dz)

        @pl.when(core == 0)
        def _():
            if layer == 0:
                load.wait()

            @pl.loop(0, NZ)
            def _(t):
                dz = step_dz(t)
                c_copy(layer, dz, 0, NX, 0).wait_recv()
                multiply(layer, dz)

    gather_multiply(0)

    def r1_copy(i):
        d = FAR_Y[i]
        return remote(
            acc.at[0, (col + d + NY) % NY], part1.at[core, -d % NY], r1_send.at[i], r1_recv.at[core], at(0, 0, 1, d)
        )

    def r1_own():
        return remote(acc.at[0, col], part1.at[0, 0], r1_send.at[7], r1_recv.at[0], sibling)

    for i in range(len(FAR_Y)):
        r1_copy(i).start()

    @pl.when(core == 0)
    def _():
        r1_own().start()

    @pl.when(core == 1)
    def _():
        part1[1, 0] = acc[0, col]
        rest = part1.at[0]
        remote(rest, rest, r1_send.at[7], r1_recv.at[0], sibling).wait_recv()
        rest = part1.at[1, pl.ds(1, 7)]
        remote(rest, rest, r1_send.at[7], r1_recv.at[1], sibling).wait_recv()
        summed = jnp.sum(part1[...], axis=1).reshape(TILE, TILE)
        hidden = jnp.maximum(summed + b1_ref[...], 0.0)
        zb[1, 0, 0] = jnp.dot(
            hidden, w2_ref[...], precision=lax.Precision.HIGHEST, preferred_element_type=jnp.float32
        ).astype(jnp.bfloat16)

    gather_multiply(1)
    part2[...] = acc[1].astype(jnp.bfloat16)

    def r2_copy(i):
        d = FAR_Y[i]
        return remote(
            part2.at[(col + d + NY) % NY], back2.at[-d % NY - 1], r2_send.at[i], r2_recv, at(0, 0, core, d)
        )

    for i in range(len(FAR_Y)):
        r2_copy(i).start()
    remote(back2, back2, r2_send.at[0], r2_recv, sibling).wait_recv()
    out_ref[...] = acc[1, col] + jnp.sum(back2[...].astype(jnp.float32), axis=0) + b2_ref[...]

    for i in range(len(FAR_Y)):
        r1_copy(i).wait_send()
        r2_copy(i).wait_send()

    @pl.when(core == 0)
    def _():
        half_copy().wait_send()
        r1_own().wait_send()

    @pl.when(core == 1)
    def _():
        for layer in range(2):
            for i in range(len(FAR_Z)):
                z_copy(layer, i).wait_send()

            @pl.loop(0, NZ)
            def _(dz):
                for i in range(len(FAR_X)):
                    x_copy(layer, dz, i).wait_send()
                c_copy(layer, dz, 0, 1, 0).wait_send()
                c_copy(layer, dz, 1, NX - 1, 1).wait_send()


def on_device(
    features, tile_coords, tile_count, tile_values, w_first, bias_first, w_second, bias_second
):
    coords = tile_coords[0, 0]
    slots = jnp.arange(SLOTS, dtype=jnp.int32)
    place = jnp.where(slots < tile_count[0, 0], coords[:, 0] * (NX * NZ) + coords[:, 1], -1)
    hit = place[:, None] == jnp.arange(RT * NX * NZ, dtype=jnp.int32)[None, :]
    slot_of = jnp.min(jnp.where(hit, slots[:, None], SLOTS), axis=0)
    vmem = pl.BlockSpec(memory_space=pltpu.VMEM)
    dma = pltpu.SemaphoreType.DMA
    return pl.pallas_call(
        kernel,
        out_shape=jax.ShapeDtypeStruct((64, TILE), jnp.float32),
        in_specs=[
            pl.BlockSpec(memory_space=pltpu.SMEM), vmem, pl.BlockSpec(memory_space=pl.ANY), vmem, vmem, vmem, vmem,
        ],
        out_specs=vmem,
        scratch_shapes=[
            pltpu.VMEM((SLOTS + 1, TILE, TILE), jnp.bfloat16),
            pltpu.VMEM((64, TILE), jnp.bfloat16),
            pltpu.VMEM((2, NZ, NX, TILE, TILE), jnp.bfloat16),
            pltpu.VMEM((2, NY, 64, TILE), jnp.float32),
            pltpu.VMEM((2, NY, 64, TILE), jnp.float32),
            pltpu.VMEM((NY, 64, TILE), jnp.bfloat16),
            pltpu.VMEM((NY - 1, 64, TILE), jnp.bfloat16),
            dma, dma, dma,
            dma((2, 11)), dma((2, NZ)), dma((2, NZ, 3)), dma((2, NZ)), dma((2, NZ, 2)), dma((2, NZ)),
            dma((8,)), dma((2,)), dma((7,)), dma,
        ],
        compiler_params=pltpu.CompilerParams(
            collective_id=0, has_side_effects=True, vmem_limit_bytes=32 * 2**20
        ),
        cost_estimate=pl.CostEstimate(flops=3 * 10**9, bytes_accessed=2 * 10**6, transcendentals=0),
    )(
        slot_of, features, tile_values[0, 0], w_first, bias_first.reshape(1, TILE), w_second, bias_second.reshape(1, TILE)
    )


def solution(mesh):
    return jax.shard_map(
        on_device,
        mesh=mesh,
        in_specs=(
            P(("row", "col"), None),
            P("row", "col", None, None),
            P("row", "col"),
            P("row", "col", None, None, None),
            P(),
            P(),
            P(),
            P(),
        ),
        out_specs=P(("row", "col"), None),
        check_vma=False,
    )
```

time: 462 us -> 78.9 us (0.17)
  waiting for transfers between devices: 401 us -> 0 us
  Pallas kernels: 0 us -> 71.2 us
  matrix products: 24.7 us -> 0 us
  between operations: 13.8 us -> 0.67 us
  local copies, waits for them, and re-layouts: 15.1 us -> 5.83 us
    all_gather x2 -> x0, waiting for transfers between devices: 250 us -> none  [aggregate(): column = lax.all_gather(node_rows, 'row', axis=0, tiled=True)]
    psum x2 -> x0, waiting for transfers between devices: 150 us -> none  [aggregate(): whole = lax.psum(summed, 'col')]
    pallas_call x0 -> x1, Pallas kernels: none -> 71.2 us  [on_device(): pl.pallas_call(kernel, out_shape=jax.ShapeDtypeStruct((64, TILE), jnp.flo...]
    dot_general x6 -> x0, matrix products: 24.7 us -> none  [the longest x2 9.59 us: aggregate(): jnp.einsum('kab,kbf->kaf', values, picked, preferred_element_type=jnp.flo...]
    dot_general x4 -> x0, local copies, waits for them, and re-layouts: 10.4 us -> none  [the longest x2 8.93 us: aggregate(): jnp.einsum('kab,kbf->kaf', values, picked, preferred_element_type=jnp.flo...]
    unnamed x8 -> x13, local copies, waits for them, and re-layouts: 0.02 us -> 5.83 us
  transfers between devices with their start and end apart: 4 -> 0, of which waited for: 4 -> 0; matrix products, arithmetic and copies ran while one was open for 0% -> 0% of each run, Pallas kernels for 0% -> 0%
where the time goes in v1:
time: 78.9 us; the launch traced here: 78.6 us
  Pallas kernels  71.2 us (90%)
  local copies, waits for them, and re-layouts  5.83 us (7%)
  other arithmetic  0.86 us (1%)
    pallas_call x1, Pallas kernels, on_device(): pl.pallas_call(kernel, out_shape=jax.ShapeDtypeStruct((64, TILE), jnp.flo...  71.2 us
    unnamed x13, local copies, waits for them, and re-layouts  5.83 us

profile of v1, /device:TPU:1, one launch (start us, length us, event | category | flops | bytes accessed | tf_op | source)
XLA Modules:
  0.0 78.6 jit_solution(9673227346895218164)
XLA Ops:
  0.7 0.8 fusion
  1.4 0.1 select_reduce_fusion.slot_ref
  1.5 0.0 copy-start
  1.5 1.5 %copy-done = bf16[1,1,54,128,128]{4,3,2,1,0:T(8,128)(2,1)S(1)} copy-done((bf16[1,1,54,128,128]{4,3,2,1,0:T(8,128)(2,1)S(1)}, bf16[1,1,54,128,128]{4,3,2,1,0:T(8,128)(2,1)}, u32[]{:S(2)}) %copy-start) | copy-done | bytes 1769496
  3.0 0.0 copy-start.1
  3.0 0.8 %copy-done.1 = f32[128,128]{1,0:T(8,128)S(1)} copy-done((f32[128,128]{1,0:T(8,128)S(1)}, f32[128,128]{1,0:T(8,128)}, u32[]{:S(2)}) %copy-start.1) | copy-done | bytes 65560
  3.8 0.0 copy-start.2
  3.8 0.8 %copy-done.2 = f32[128,128]{1,0:T(8,128)S(1)} copy-done((f32[128,128]{1,0:T(8,128)S(1)}, f32[128,128]{1,0:T(8,128)}, u32[]{:S(2)}) %copy-start.2) | copy-done | bytes 65560
  4.7 0.0 copy-start.3
  4.7 0.8 copy-done.3
  5.4 0.0 copy-start.4
  5.4 0.7 copy-done.4
  6.1 0.0 copy-start.5
  6.1 0.7 copy-done.5
  6.7 71.2 %shard_map.82 = f32[64,128]{1,0:T(8,128)S(1)} custom-call(s32[192]{0:T(256)S(1)} %select_reduce_fusion.slot_ref, f32[64,128]{1,0:T(8,128)S(1)} %copy-done.3, bf16[54,128,128]{2,1,0:T(8,128)(2,1)S(1)} %bitcast.8, f32[128,128]{1,0:T(8,128)S(1)} %copy-done.1, f32[1,128]{1,0:T(1,128)S(1)} %bitcast.9, f32[128,128]{1,0:T(8,128)S(1)} %copy-done.2, ...), custom_call_target="tpu_custom_call" | custom-call | flops 3000000000 | bytes 2000000 | tf_op jit(solution)/shard_map/pallas_call | solution.py:237
  78.0 0.6 copy.11
Async XLA Ops:
  1.5 1.5 %copy-start = (bf16[1,1,54,128,128]{4,3,2,1,0:T(8,128)(2,1)S(1)}, bf16[1,1,54,128,128]{4,3,2,1,0:T(8,128)(2,1)}, u32[]{:S(2)}) copy-start(bf16[1,1,54,128,128]{4,3,2,1,0:T(8,128)(2,1)} %param.11) | copy-start | bytes 5308420
  3.0 0.8 %copy-start.1 = (f32[128,128]{1,0:T(8,128)S(1)}, f32[128,128]{1,0:T(8,128)}, u32[]{:S(2)}) copy-start(f32[128,128]{1,0:T(8,128)} %w1_ref.1) | copy-start | bytes 196612
  3.8 0.8 %copy-start.2 = (f32[128,128]{1,0:T(8,128)S(1)}, f32[128,128]{1,0:T(8,128)}, u32[]{:S(2)}) copy-start(f32[128,128]{1,0:T(8,128)} %w2_ref.1) | copy-start | bytes 196612
  4.7 0.8 copy-start.3
  5.4 0.7 copy-start.4
  6.1 0.7 copy-start.5

commit v2 on v0

v2 whole, which is shorter than its diff:
```python
import jax
import jax.numpy as jnp
from jax import lax
from jax.experimental import pallas as pl
from jax.experimental.pallas import tpu as pltpu
from jax.sharding import PartitionSpec as P

MESH = pl.DeviceIdType.MESH
NX, NZ, NY = 4, 12, 8
TILE, RT, SLOTS, NODE = 128, 4, 54, 64
SEND_Z = (2, -2, 6, 5, -5, 4, -4, 3, -3, 1, -1)
FAR_X = (2, 1, -1)
FAR_Y = (4, 3, -3, 2, -2, 1, -1)
NEAR_Z = (1, NZ - 1)
BY_Z = (2, 10, 3, 9, 4, 8, 5, 7, 6)
GROUPS = (0, 2, 10, 3, 9, 1, 11, 4, 8, 5, 7, 6)
LAG = 3
WIDE_Y, NARROW_Y = (2, -2, 1, -1), (4, 3, -3)


def kernel(
    count_ref, coords_hbm, feat_hbm, tiles_hbm, w1_hbm, b1_hbm, w2_hbm, b2_hbm, out_ref,
    coords, feat, tiles, w1, b1, w2, b2, table_v, table, zb, acc, wide, narrow, part2, back2,
    load_sem, table_sem, z_send, z_recv, zx_send, x_send, x_recv, c_send, c_recv,
    r1_send, r1_recv, r2_send, r2_recv,
):
    row, col = lax.axis_index("row"), lax.axis_index("col")
    core = row % 2
    chip = row // 2
    z, x = chip % NZ, chip // NZ

    def at(dx, dz, c, dy=0):
        return (
            (((x + dx + NX) % NX) * NZ + (z + dz + NZ) % NZ) * 2 + c,
            (col + dy + NY) % NY,
        )

    def remote(src, dst, send, recv, to):
        return pltpu.make_async_remote_copy(
            src_ref=src, dst_ref=dst, send_sem=send, recv_sem=recv, device_id=to, device_id_type=MESH
        )

    sibling = at(0, 0, 1 - core)

    loads = [
        pltpu.make_async_copy(src, dst, load_sem.at[i])
        for i, (src, dst) in enumerate(
            (
                (feat_hbm, feat), (w1_hbm, w1), (coords_hbm, coords),
                (tiles_hbm, tiles.at[pl.ds(0, SLOTS)]), (b1_hbm, b1), (w2_hbm, w2), (b2_hbm, b2),
            )
        )
    ]
    for load in loads:
        load.start()

    barrier = pltpu.get_barrier_semaphore()
    peers = [at(0, d, core) for d in SEND_Z] + [at(0, 0, core, d) for d in FAR_Y]
    peers += [at(d, 0, core) for d in FAR_X] + [sibling]
    for to in peers:
        pl.semaphore_signal(barrier, inc=1, device_id=to, device_id_type=MESH)

    loads[0].wait()
    loads[1].wait()
    zb[0, 0, 0, core] = jnp.dot(
        feat[...], w1[...], precision=lax.Precision.HIGHEST, preferred_element_type=jnp.float32
    ).astype(jnp.bfloat16)

    pl.semaphore_wait(barrier, len(peers))

    def z_copy(layer, i):
        d = SEND_Z[i]
        return remote(
            zb.at[layer, 0, 0, core], zb.at[layer, -d % NZ, 0, core],
            z_send.at[layer, i], z_recv.at[layer, -d % NZ], at(0, d, core),
        )

    def x_copy(layer, dz, i):
        d = FAR_X[i]
        return remote(
            zb.at[layer, dz, 0, core], zb.at[layer, dz, -d % NX, core],
            x_send.at[layer, dz, i], x_recv.at[layer, dz], at(d, 0, core),
        )

    def c_copy(layer, dz, i):
        block = zb.at[layer, dz, pl.ds(1, NX - 1) if i else 0, core]
        return remote(block, block, c_send.at[layer, dz, i], c_recv.at[layer, dz], sibling)

    def multiply(layer, dz):
        za = (z + dz) % NZ
        places = [((x + dx) % NX) * NZ + za for dx in range(NX)]
        rhs = zb[layer, dz].reshape(NX * TILE, TILE)
        for r in range(RT):
            lhs = jnp.concatenate(
                [tiles[table[0, r * NX * NZ + p]] for p in places], axis=1
            )
            acc[layer, 2 * r : 2 * r + 2] += jnp.dot(
                lhs, rhs, preferred_element_type=jnp.float32
            ).reshape(2, NODE, TILE)

    def pass_x_on(layer, i):
        d = (1, -1)[i]
        return remote(
            zb.at[layer, 0, pl.ds(1, NX - 1), core], zb.at[layer, -d % NZ, pl.ds(1, NX - 1), core],
            zx_send.at[layer, i], x_recv.at[layer, -d % NZ], at(0, d, core),
        )

    def arrived(block, recv):
        remote(block, block, z_send.at[0, 0], recv, sibling).wait_recv()

    def start_gather(layer):
        for i in range(len(FAR_X)):
            x_copy(layer, 0, i).start()
        for i in range(len(SEND_Z)):
            z_copy(layer, i).start()
        c_copy(layer, 0, 0).start()
        acc[layer] = jnp.zeros((NY, NODE, TILE), jnp.float32)

    def take_z(layer, dz):
        arrived(zb.at[layer, dz, 0, core], z_recv.at[layer, dz])
        if dz not in NEAR_Z:
            for i in range(len(FAR_X)):
                x_copy(layer, dz, i).start()
        c_copy(layer, dz, 0).start()

    def take_x(layer, dz):
        arrived(zb.at[layer, dz, pl.ds(1, NX - 1), core], x_recv.at[layer, dz])
        if dz == 0:
            for i in range(2):
                pass_x_on(layer, i).start()
        c_copy(layer, dz, 1).start()

    def use(layer, dz):
        arrived(zb.at[layer, dz, :, 1 - core], c_recv.at[layer, dz])
        multiply(layer, dz)

    def gather_multiply(layer):
        take_z(layer, BY_Z[0])
        take_z(layer, BY_Z[1])
        take_x(layer, 0)
        for dz in BY_Z[2:] + NEAR_Z:
            take_z(layer, dz)
        for t in range(1, NZ + LAG):
            if t < NZ:
                take_x(layer, GROUPS[t])
            if t >= LAG:
                use(layer, GROUPS[t - LAG])

    def drain(layer):
        for i in range(len(SEND_Z)):
            z_copy(layer, i).wait_send()
        for i in range(2):
            pass_x_on(layer, i).wait_send()
        for dz in range(NZ):
            for i in range(len(FAR_X) if dz not in NEAR_Z else 0):
                x_copy(layer, dz, i).wait_send()
            for i in range(2):
                c_copy(layer, dz, i).wait_send()

    start_gather(0)
    loads[2].wait()
    lane = lax.broadcasted_iota(jnp.int32, (SLOTS, SLOTS), 1)
    slot = lax.broadcasted_iota(jnp.int32, (SLOTS, SLOTS), 0)
    place = coords[0:1, :] * (NX * NZ) + coords[1:2, :]
    place = jnp.where(lane[0:1] < count_ref[0, 0], place, -1)
    place = jnp.max(jnp.where(lane == slot, place, -1), axis=1, keepdims=True)
    hit = place == lax.broadcasted_iota(jnp.int32, (SLOTS, 2 * TILE), 1)
    used = jnp.where(hit, lax.broadcasted_iota(jnp.int32, (SLOTS, 2 * TILE), 0), SLOTS)
    table_v[...] = jnp.min(used, axis=0, keepdims=True)
    to_table = pltpu.make_async_copy(table_v, table, table_sem)
    to_table.start()
    tiles[SLOTS] = jnp.zeros((TILE, TILE), jnp.bfloat16)
    for load in loads[3:]:
        load.wait()
    to_table.wait()
    gather_multiply(0)

    def wide_copy(i):
        d = WIDE_Y[i]
        return remote(
            acc.at[0, (col + d + NY) % NY], wide.at[WIDE_Y.index(-d)], r1_send.at[i], r1_recv.at[0], at(0, 0, core, d)
        )

    def narrow_copy(i):
        d = NARROW_Y[i]
        slot = (0, 2, 1)[i]
        return remote(narrow.at[0, i], narrow.at[1, slot], r1_send.at[4 + i], r1_recv.at[1], at(0, 0, core, d))

    for i, d in enumerate(NARROW_Y):
        narrow[0, i] = acc[0, (col + d + NY) % NY].astype(jnp.bfloat16)
        narrow_copy(i).start()
    for i in range(len(WIDE_Y)):
        wide_copy(i).start()
    total = acc[0, col] + b1[...]
    arrived(wide, r1_recv.at[0])
    total += jnp.sum(wide[...], axis=0)
    arrived(narrow.at[1], r1_recv.at[1])
    total += jnp.sum(narrow[1].astype(jnp.float32), axis=0)
    hidden = jnp.maximum(total, 0.0)
    zb[1, 0, 0, core] = jnp.dot(
        hidden, w2[...], precision=lax.Precision.HIGHEST, preferred_element_type=jnp.float32
    ).astype(jnp.bfloat16)

    start_gather(1)
    gather_multiply(1)
    part2[...] = acc[1].astype(jnp.bfloat16)

    def r2_copy(i):
        d = FAR_Y[i]
        return remote(
            part2.at[(col + d + NY) % NY], back2.at[-d % NY - 1], r2_send.at[i], r2_recv, at(0, 0, core, d)
        )

    for i in range(len(FAR_Y)):
        r2_copy(i).start()

    for i in range(len(WIDE_Y)):
        wide_copy(i).wait_send()
    for i in range(len(NARROW_Y)):
        narrow_copy(i).wait_send()
    drain(0)
    drain(1)

    own = acc[1, col] + b2[...]
    arrived(back2, r2_recv)
    out_ref[...] = own + jnp.sum(back2[...].astype(jnp.float32), axis=0)
    for i in range(len(FAR_Y)):
        r2_copy(i).wait_send()


def on_device(
    features, tile_coords, tile_count, tile_values, w_first, bias_first, w_second, bias_second
):
    hbm = pl.BlockSpec(memory_space=pltpu.HBM)
    dma = pltpu.SemaphoreType.DMA
    bf16, f32, i32 = jnp.bfloat16, jnp.float32, jnp.int32
    in_hbm = (
        tile_coords[0, 0].T, features, tile_values[0, 0],
        w_first, bias_first.reshape(1, TILE), w_second, bias_second.reshape(1, TILE),
    )
    return pl.pallas_call(
        kernel,
        out_shape=jax.ShapeDtypeStruct((NODE, TILE), f32),
        in_specs=[pl.BlockSpec(memory_space=pltpu.SMEM)] + [hbm] * 7,
        out_specs=pl.BlockSpec(memory_space=pltpu.VMEM),
        scratch_shapes=[
            pltpu.VMEM((2, SLOTS), i32),
            pltpu.VMEM((NODE, TILE), f32),
            pltpu.VMEM((SLOTS + 1, TILE, TILE), bf16),
            pltpu.VMEM((TILE, TILE), f32),
            pltpu.VMEM((1, TILE), f32),
            pltpu.VMEM((TILE, TILE), f32),
            pltpu.VMEM((1, TILE), f32),
            pltpu.VMEM((1, 2 * TILE), i32),
            pltpu.SMEM((1, 2 * TILE), i32),
            pltpu.VMEM((2, NZ, NX, 2, NODE, TILE), bf16),
            pltpu.VMEM((2, NY, NODE, TILE), f32),
            pltpu.VMEM((4, NODE, TILE), f32),
            pltpu.VMEM((2, 3, NODE, TILE), bf16),
            pltpu.VMEM((NY, NODE, TILE), bf16),
            pltpu.VMEM((NY - 1, NODE, TILE), bf16),
            dma((7,)), dma,
            dma((2, 11)), dma((2, NZ)), dma((2, 2)), dma((2, NZ, 3)), dma((2, NZ)), dma((2, NZ, 2)), dma((2, NZ)),
            dma((7,)), dma((2,)), dma((7,)), dma,
        ],
        compiler_params=pltpu.CompilerParams(
            collective_id=0, has_side_effects=True, vmem_limit_bytes=48 * 2**20
        ),
        cost_estimate=pl.CostEstimate(flops=3 * 10**9, bytes_accessed=2 * 10**6, transcendentals=0),
    )(tile_count, *[pltpu.with_memory_space_constraint(a, pltpu.HBM) for a in in_hbm])


def solution(mesh):
    return jax.shard_map(
        on_device,
        mesh=mesh,
        in_specs=(
            P(("row", "col"), None),
            P("row", "col", None, None),
            P("row", "col"),
            P("row", "col", None, None, None),
            P(),
            P(),
            P(),
            P(),
        ),
        out_specs=P(("row", "col"), None),
        check_vma=False,
    )
```

time: 462 us -> 68.5 us (0.15)
  waiting for transfers between devices: 401 us -> 0 us
  Pallas kernels: 0 us -> 67.1 us
  matrix products: 24.7 us -> 0 us
  local copies, waits for them, and re-layouts: 15.1 us -> 0.62 us
  between operations: 13.8 us -> 0.66 us
    all_gather x2 -> x0, waiting for transfers between devices: 250 us -> none  [aggregate(): column = lax.all_gather(node_rows, 'row', axis=0, tiled=True)]
    psum x2 -> x0, waiting for transfers between devices: 150 us -> none  [aggregate(): whole = lax.psum(summed, 'col')]
    pallas_call x0 -> x1, Pallas kernels: none -> 67.1 us  [on_device(): pl.pallas_call(kernel, out_shape=jax.ShapeDtypeStruct((NODE, TILE), f32),...]
    dot_general x6 -> x0, matrix products: 24.7 us -> none  [the longest x2 9.59 us: aggregate(): jnp.einsum('kab,kbf->kaf', values, picked, preferred_element_type=jnp.flo...]
    dot_general x4 -> x0, local copies, waits for them, and re-layouts: 10.4 us -> none  [the longest x2 8.93 us: aggregate(): jnp.einsum('kab,kbf->kaf', values, picked, preferred_element_type=jnp.flo...]
  transfers between devices with their start and end apart: 4 -> 0, of which waited for: 4 -> 0; matrix products, arithmetic and copies ran while one was open for 0% -> 0% of each run, Pallas kernels for 0% -> 0%
where the time goes in v2:
time: 68.5 us; the launch traced here: 68.3 us
  Pallas kernels  67.1 us (98%)
    pallas_call x1, Pallas kernels, on_device(): pl.pallas_call(kernel, out_shape=jax.ShapeDtypeStruct((NODE, TILE), f32),...  67.1 us

profile of v2, /device:TPU:1, one launch (start us, length us, event | category | flops | bytes accessed | tf_op | source)
XLA Modules:
  0.0 68.3 jit_solution(8037365954241525967)
XLA Ops:
  0.7 67.1 %shard_map.82 = f32[64,128]{1,0:T(8,128)S(1)} custom-call(s32[1,1]{1,0:T(1,128)S(6)} %copy.10.count_ref, s32[2,54]{1,0:T(2,128)} %bitcast.7, f32[64,128]{1,0:T(8,128)} %feat_hbm.1, bf16[54,128,128]{2,1,0:T(8,128)(2,1)} %bitcast.6, f32[128,128]{1,0:T(8,128)} %w1_hbm.1, f32[1,128]{1,0:T(1,128)} %bitcast.8, f32[128,128]{1,0:T(8,128)} %w2_hbm.1, f32[1,128]{1,0:T(1,128)} %bitcast.9), custom_call_target="tpu_custom_call" | custom-call | flops 3000000000 | bytes 2000000 | tf_op jit(solution)/shard_map/pallas_call | solution.py:241
  67.7 0.6 copy.11

commit v3 on v2

v3 whole, which is shorter than its diff:
```python
import jax
import jax.numpy as jnp
from jax import lax
from jax.experimental import pallas as pl
from jax.experimental.pallas import tpu as pltpu
from jax.sharding import PartitionSpec as P

MESH = pl.DeviceIdType.MESH
NX, NZ, NY = 4, 12, 8
TILE, RT, SLOTS, NODE = 128, 4, 54, 64
SEND_Z = (2, -2, 3, -3, 4, -4, 5, -5, 6, 1, -1)
TAKE_Z = (2, -2, 3, -3, 4, -4, 5, -5, 6, 1, -1)
NEAR_Z = (1, -1)
EARLY = (0, 2, -2)
GROUPS = (0, 2, -2, 3, -3, 1, -1, 4, -4, 5, -5, 6)
RANK = {d: k for k, d in enumerate(GROUPS)} | {-6: GROUPS.index(6)}
LAG = 3
WIDE_Y, NARROW_Y = (1, -1), (4, 3, -3, 2, -2)
FAR_Y = (4, 3, -3, 2, -2, 1, -1)


def kernel(
    count_ref, coords_hbm, feat_hbm, tiles_hbm, w1_hbm, b1_hbm, w2_hbm, b2_hbm, out_ref,
    coords, feat, tiles, w1, b1, w2, b2, table_v, table, half, zb, acc, wide, narrow, narrow_out, own0, part2, back2,
    load_sem, table_sem, half_send, half_recv, z_send, z_recv, zx_send, x_send, x_recv, c_send, c_recv,
    r1_send, r1_recv, own_send, own_recv, r2_send, r2_recv,
):
    row, col = lax.axis_index("row"), lax.axis_index("col")
    core = row % 2
    chip = row // 2
    z, x = chip % NZ, chip // NZ

    def at(dx, dz, c, dy=0):
        return (
            (((x + dx + NX) % NX) * NZ + (z + dz + NZ) % NZ) * 2 + c,
            (col + dy + NY) % NY,
        )

    def remote(src, dst, send, recv, to):
        return pltpu.make_async_remote_copy(
            src_ref=src, dst_ref=dst, send_sem=send, recv_sem=recv, device_id=to, device_id_type=MESH
        )

    def arrived(block, recv):
        remote(block, block, z_send.at[0, 0], recv, sibling).wait_recv()

    loads = [
        pltpu.make_async_copy(src, dst, load_sem.at[i])
        for i, (src, dst) in enumerate(
            (
                (feat_hbm, feat), (w1_hbm, w1), (coords_hbm, coords),
                (tiles_hbm, tiles.at[pl.ds(0, SLOTS)]), (b1_hbm, b1), (w2_hbm, w2), (b2_hbm, b2),
            )
        )
    ]
    for load in loads[:2]:
        load.start()

    sibling = at(0, 0, 1 - core)
    barrier = pltpu.get_barrier_semaphore()

    def signal(to):
        pl.semaphore_signal(barrier, inc=1, device_id=to, device_id_type=MESH)

    @pl.when(core == 0)
    def _():
        for d in (6, 5, -5, 4, -4, 3, -3, 2, -2, 1, -1):
            signal(at(0, d, 1))

    @pl.when(core == 1)
    def _():
        for d in FAR_Y:
            signal(at(0, 0, 1, d))
        for d in (2, 1, -1):
            signal(at(d, 0, 0))
        signal(at(2, 0, 1))
        for d in NEAR_Z:
            signal(at(0, d, 1))

    signal(sibling)
    for d in FAR_Y:
        signal(at(0, 0, 0, d))

    for load in loads[2:]:
        load.start()
    loads[0].wait()
    loads[1].wait()
    mixed = jnp.dot(
        feat[...], w1[...], precision=lax.Precision.HIGHEST, preferred_element_type=jnp.float32
    ).astype(jnp.bfloat16)

    def half_copy():
        return remote(half, zb.at[0, 0, 0, pl.ds(0, NODE)], half_send, half_recv, sibling)

    def z_copy(layer, i):
        d = SEND_Z[i]
        return remote(
            zb.at[layer, 0, 0], zb.at[layer, RANK[-d], 0],
            z_send.at[layer, i], z_recv.at[layer, RANK[-d]], at(0, d, 0),
        )

    def x_copy(layer, dz, d):
        k, i = RANK[dz], d % NX - 1
        return remote(
            zb.at[layer, k, 0], zb.at[layer, k, -d % NX],
            x_send.at[layer, k, i], x_recv.at[layer, k], at(d, 0, 1),
        )

    def pass_x_on(layer, i):
        d = NEAR_Z[i]
        return remote(
            zb.at[layer, 0, pl.ds(1, NX - 1)], zb.at[layer, RANK[-d], pl.ds(1, NX - 1)],
            zx_send.at[layer, i], x_recv.at[layer, RANK[-d]], at(0, d, 1),
        )

    def c_one(layer, dz):
        block = zb.at[layer, RANK[dz], 0]
        return remote(block, block, c_send.at[layer, RANK[dz], 0], c_recv.at[layer, RANK[dz], 0], sibling)

    def c_rest(layer, dz):
        block = zb.at[layer, RANK[dz], pl.ds(1, NX - 1)]
        return remote(block, block, c_send.at[layer, RANK[dz], 1], c_recv.at[layer, RANK[dz], 1], sibling)

    def multiply(layer, dz):
        za = (z + dz + NZ) % NZ
        places = [((x + dx) % NX) * NZ + za for dx in range(NX)]
        rhs = zb[layer, RANK[dz]].reshape(NX * TILE, TILE)
        for r in range(RT):
            lhs = jnp.concatenate(
                [tiles[table[0, r * NX * NZ + p]] for p in places], axis=1
            )
            acc[layer, 2 * r : 2 * r + 2] += jnp.dot(
                lhs, rhs, preferred_element_type=jnp.float32
            ).reshape(2, NODE, TILE)

    def start_gather(layer):
        c_one(layer, 0).start()
        for i in range(len(SEND_Z)):
            z_copy(layer, i).start()

    def sends_of_x(dz):
        return (2, 1, -1) if dz in EARLY else (1, -1)

    def gather_0(layer):
        arrived(zb.at[layer, 0, 0], c_recv.at[layer, 0, 0])
        for d in sends_of_x(0):
            x_copy(layer, 0, d).start()
        for dz in TAKE_Z:
            arrived(zb.at[layer, RANK[dz], 0], z_recv.at[layer, RANK[dz]])
            if dz not in NEAR_Z:
                for d in sends_of_x(dz):
                    x_copy(layer, dz, d).start()
            c_one(layer, dz).start()
        for dz in GROUPS:
            arrived(zb.at[layer, RANK[dz], pl.ds(1, NX - 1)], c_recv.at[layer, RANK[dz], 1])
            multiply(layer, dz)

    def take_c(layer, dz):
        arrived(zb.at[layer, RANK[dz], 0], c_recv.at[layer, RANK[dz], 0])
        if dz not in NEAR_Z + EARLY:
            x_copy(layer, dz, 2).start()

    def take_x(layer, dz):
        arrived(zb.at[layer, RANK[dz], pl.ds(1, NX - 1)], x_recv.at[layer, RANK[dz]])
        if dz == 0:
            for i in range(2):
                pass_x_on(layer, i).start()
        c_rest(layer, dz).start()

    def gather_1(layer):
        for dz in (2, -2, 3, -3):
            take_c(layer, dz)
        take_x(layer, 0)
        for dz in TAKE_Z[4:]:
            take_c(layer, dz)
        for t in range(1, NZ + LAG):
            if t < NZ:
                take_x(layer, GROUPS[t])
            if t >= LAG:
                multiply(layer, GROUPS[t - LAG])

    def drain_0(layer):
        for dz in GROUPS:
            if dz not in NEAR_Z:
                for d in sends_of_x(dz):
                    x_copy(layer, dz, d).wait_send()
            if dz != 0:
                c_one(layer, dz).wait_send()

    def drain_1(layer):
        c_one(layer, 0).wait_send()
        for i in range(len(SEND_Z)):
            z_copy(layer, i).wait_send()
        for i in range(2):
            pass_x_on(layer, i).wait_send()
        for dz in GROUPS:
            if dz not in NEAR_Z + EARLY:
                x_copy(layer, dz, 2).wait_send()
            c_rest(layer, dz).wait_send()

    @pl.when(core == 0)
    def _():
        half[...] = mixed
        pl.semaphore_wait(barrier, 3 + 1 + 7 + 7)
        half_copy().start()

    @pl.when(core == 1)
    def _():
        zb[0, 0, 0, NODE:TILE] = mixed
        pl.semaphore_wait(barrier, 11 + 2 + 1 + 1 + 7)
        half_copy().wait_recv()
        start_gather(0)

    loads[2].wait()
    lane = lax.broadcasted_iota(jnp.int32, (SLOTS, SLOTS), 1)
    slot = lax.broadcasted_iota(jnp.int32, (SLOTS, SLOTS), 0)
    place = coords[0:1, :] * (NX * NZ) + coords[1:2, :]
    place = jnp.where(lane[0:1] < count_ref[0, 0], place, -1)
    place = jnp.max(jnp.where(lane == slot, place, -1), axis=1, keepdims=True)
    hit = place == lax.broadcasted_iota(jnp.int32, (SLOTS, 2 * TILE), 1)
    used = jnp.where(hit, lax.broadcasted_iota(jnp.int32, (SLOTS, 2 * TILE), 0), SLOTS)
    table_v[...] = jnp.min(used, axis=0, keepdims=True)
    to_table = pltpu.make_async_copy(table_v, table, table_sem)
    to_table.start()
    tiles[SLOTS] = jnp.zeros((TILE, TILE), jnp.bfloat16)
    acc[...] = jnp.zeros((2, NY, NODE, TILE), jnp.float32)
    for load in loads[3:]:
        load.wait()
    to_table.wait()

    def wide_copy(i):
        d = WIDE_Y[i]
        return remote(
            acc.at[0, (col + d + NY) % NY], wide.at[core, WIDE_Y.index(-d)],
            r1_send.at[i], r1_recv.at[core, 0], at(0, 0, 1, d),
        )

    def narrow_copy(i):
        d = NARROW_Y[i]
        return remote(
            narrow_out.at[i], narrow.at[core, NARROW_Y.index(d if d == 4 else -d)],
            r1_send.at[len(WIDE_Y) + i], r1_recv.at[core, 1], at(0, 0, 1, d),
        )

    def own_copy():
        return remote(acc.at[0, col], own0, own_send, own_recv, sibling)

    def send_partials():
        for i, d in enumerate(NARROW_Y):
            narrow_out[i] = acc[0, (col + d + NY) % NY].astype(jnp.bfloat16)
            narrow_copy(i).start()
        for i in range(len(WIDE_Y)):
            wide_copy(i).start()

    @pl.when(core == 0)
    def _():
        gather_0(0)
        send_partials()
        own_copy().start()
        gather_0(1)

    @pl.when(core == 1)
    def _():
        gather_1(0)
        send_partials()
        own = acc[0, col] + b1[...]
        arrived(own0, own_recv)
        totals = [own0[...] + b1[...], own]
        for c in (1, 0):
            arrived(wide.at[c], r1_recv.at[c, 0])
            totals[c] += jnp.sum(wide[c], axis=0)
            arrived(narrow.at[c], r1_recv.at[c, 1])
            totals[c] += jnp.sum(narrow[c].astype(jnp.float32), axis=0)
        hidden = jnp.maximum(jnp.concatenate(totals, axis=0), 0.0)
        zb[1, 0, 0] = jnp.dot(
            hidden, w2[...], precision=lax.Precision.HIGHEST, preferred_element_type=jnp.float32
        ).astype(jnp.bfloat16)
        start_gather(1)
        gather_1(1)

    part2[...] = acc[1].astype(jnp.bfloat16)

    def r2_copy(i):
        d = FAR_Y[i]
        return remote(
            part2.at[(col + d + NY) % NY], back2.at[-d % NY - 1], r2_send.at[i], r2_recv, at(0, 0, core, d)
        )

    for i in range(len(FAR_Y)):
        r2_copy(i).start()

    for i in range(len(WIDE_Y)):
        wide_copy(i).wait_send()
    for i in range(len(NARROW_Y)):
        narrow_copy(i).wait_send()

    @pl.when(core == 0)
    def _():
        half_copy().wait_send()
        own_copy().wait_send()
        drain_0(0)
        drain_0(1)

    @pl.when(core == 1)
    def _():
        drain_1(0)
        drain_1(1)

    own = acc[1, col] + b2[...]
    arrived(back2, r2_recv)
    out_ref[...] = own + jnp.sum(back2[...].astype(jnp.float32), axis=0)
    for i in range(len(FAR_Y)):
        r2_copy(i).wait_send()


def on_device(
    features, tile_coords, tile_count, tile_values, w_first, bias_first, w_second, bias_second
):
    hbm = pl.BlockSpec(memory_space=pltpu.HBM)
    dma = pltpu.SemaphoreType.DMA
    bf16, f32, i32 = jnp.bfloat16, jnp.float32, jnp.int32
    in_hbm = (
        tile_coords[0, 0].T, features, tile_values[0, 0],
        w_first, bias_first.reshape(1, TILE), w_second, bias_second.reshape(1, TILE),
    )
    return pl.pallas_call(
        kernel,
        out_shape=jax.ShapeDtypeStruct((NODE, TILE), f32),
        in_specs=[pl.BlockSpec(memory_space=pltpu.SMEM)] + [hbm] * 7,
        out_specs=pl.BlockSpec(memory_space=pltpu.VMEM),
        scratch_shapes=[
            pltpu.VMEM((2, SLOTS), i32),
            pltpu.VMEM((NODE, TILE), f32),
            pltpu.VMEM((SLOTS + 1, TILE, TILE), bf16),
            pltpu.VMEM((TILE, TILE), f32),
            pltpu.VMEM((1, TILE), f32),
            pltpu.VMEM((TILE, TILE), f32),
            pltpu.VMEM((1, TILE), f32),
            pltpu.VMEM((1, 2 * TILE), i32),
            pltpu.SMEM((1, 2 * TILE), i32),
            pltpu.VMEM((NODE, TILE), bf16),
            pltpu.VMEM((2, NZ, NX, TILE, TILE), bf16),
            pltpu.VMEM((2, NY, NODE, TILE), f32),
            pltpu.VMEM((2, 2, NODE, TILE), f32),
            pltpu.VMEM((2, 5, NODE, TILE), bf16),
            pltpu.VMEM((5, NODE, TILE), bf16),
            pltpu.VMEM((NODE, TILE), f32),
            pltpu.VMEM((NY, NODE, TILE), bf16),
            pltpu.VMEM((NY - 1, NODE, TILE), bf16),
            dma((7,)), dma, dma, dma,
            dma((2, 11)), dma((2, NZ)), dma((2, 2)), dma((2, NZ, 3)), dma((2, NZ)), dma((2, NZ, 2)), dma((2, NZ, 2)),
            dma((7,)), dma((2, 2)), dma, dma, dma((7,)), dma,
        ],
        compiler_params=pltpu.CompilerParams(
            collective_id=0, has_side_effects=True, vmem_limit_bytes=48 * 2**20
        ),
        cost_estimate=pl.CostEstimate(flops=3 * 10**9, bytes_accessed=2 * 10**6, transcendentals=0),
    )(tile_count, *[pltpu.with_memory_space_constraint(a, pltpu.HBM) for a in in_hbm])


def solution(mesh):
    return jax.shard_map(
        on_device,
        mesh=mesh,
        in_specs=(
            P(("row", "col"), None),
            P("row", "col", None, None),
            P("row", "col"),
            P("row", "col", None, None, None),
            P(),
            P(),
            P(),
            P(),
        ),
        out_specs=P(("row", "col"), None),
        check_vma=False,
    )
```

time: 68.5 us -> 65.2 us (0.952)
  Pallas kernels: 67.1 us -> 63.3 us
    pallas_call x1, Pallas kernels: 67.1 us -> 63.3 us  [on_device(): pl.pallas_call(kernel, out_shape=jax.ShapeDtypeStruct((NODE, TILE), f32),...]
where the time goes in v3:
time: 65.2 us; the launch traced here: 64.6 us
  Pallas kernels  63.3 us (97%)
  between operations  0.66 us (1%)
    pallas_call x1, Pallas kernels, on_device(): pl.pallas_call(kernel, out_shape=jax.ShapeDtypeStruct((NODE, TILE), f32),...  63.3 us

profile of v3, /device:TPU:1, one launch (start us, length us, event | category | flops | bytes accessed | tf_op | source)
XLA Modules:
  0.0 64.6 jit_solution(15903472685244012075)
XLA Ops:
  0.7 63.3 %shard_map.82 = f32[64,128]{1,0:T(8,128)S(1)} custom-call(s32[1,1]{1,0:T(1,128)S(6)} %copy.10.count_ref, s32[2,54]{1,0:T(2,128)} %bitcast.7, f32[64,128]{1,0:T(8,128)} %feat_hbm.1, bf16[54,128,128]{2,1,0:T(8,128)(2,1)} %bitcast.6, f32[128,128]{1,0:T(8,128)} %w1_hbm.1, f32[1,128]{1,0:T(1,128)} %bitcast.8, f32[128,128]{1,0:T(8,128)} %w2_hbm.1, f32[1,128]{1,0:T(1,128)} %bitcast.9), custom_call_target="tpu_custom_call" | custom-call | flops 3000000000 | bytes 2000000 | tf_op jit(solution)/shard_map/pallas_call | solution.py:326
  63.9 0.6 copy.11

commit v4 on v2

v4 whole, which is shorter than its diff:
```python
import functools

import jax
import jax.numpy as jnp
from jax import lax
from jax.experimental import pallas as pl
from jax.experimental.pallas import tpu as pltpu
from jax.sharding import PartitionSpec as P

MESH = pl.DeviceIdType.MESH
NX, NZ, NY = 4, 12, 8
TILE, RT, SLOTS, NODE = 128, 4, 54, 64
OPT = dict(
    nl=2,
    SEND_Z=(2, -2, 3, -3, 4, -4, 5, -5, 6, 1, -1),
    BY_Z=(2, -2, 3, -3, 4, -4, 5, -5, 6),
    ZCOUNT=4,
    BUNDLES=((0,), (2,), (-2,), (3,), (-3,), (4,), (-4,), (1,), (-1,), (5,), (-5,), (6,)),
    LAG=6,
    X=(2, 1, -1),
    WIDE_Y=(), NARROW_Y=(4, 3, -3, 2, -2, 1, -1),
)


def kernel(
    opt,
    count_ref, coords_hbm, feat_hbm, tiles_hbm, w1_hbm, b1_hbm, w2_hbm, b2_hbm, out_ref,
    coords, feat, tiles, w1, b1, w2, b2, table_v, table, zb, acc, wide, narrow, part2, back2,
    load_sem, table_sem, z_send, z_recv, zx_send, x_send, x_recv, c_send, c_recv,
    r1_send, r1_recv, r2_send, r2_recv,
):
    nl, SEND_Z, BY_Z, BUNDLES, LAG, FAR_X = opt["nl"], opt["SEND_Z"], opt["BY_Z"], opt["BUNDLES"], opt["LAG"], opt["X"]
    WIDE_Y, NARROW_Y = opt["WIDE_Y"], opt["NARROW_Y"]
    NEAR_Z = (1, -1)
    order = [d for b in BUNDLES for d in b]
    rank = {d: k for k, d in enumerate(order)}
    rank[-6] = rank[6]
    row, col = lax.axis_index("row"), lax.axis_index("col")
    core = row % 2
    chip = row // 2
    z, x = chip % NZ, chip // NZ

    def at(dx, dz, c, dy=0):
        return (
            (((x + dx + NX) % NX) * NZ + (z + dz + NZ) % NZ) * 2 + c,
            (col + dy + NY) % NY,
        )

    def remote(src, dst, send, recv, to):
        return pltpu.make_async_remote_copy(
            src_ref=src, dst_ref=dst, send_sem=send, recv_sem=recv, device_id=to, device_id_type=MESH
        )

    sibling = at(0, 0, 1 - core)

    barrier = pltpu.get_barrier_semaphore()
    peers = [at(0, d, core) for d in (6, 5, -5, 4, -4)] + [at(0, 0, core, d) for d in (4, 3, -3)]
    peers += [at(0, d, core) for d in (3, -3, 2, -2, 1, -1)] + [at(0, 0, core, d) for d in (2, -2, 1, -1)]
    peers += [at(d, 0, core) for d in FAR_X] + [sibling]
    for to in peers:
        pl.semaphore_signal(barrier, inc=1, device_id=to, device_id_type=MESH)

    loads = [
        pltpu.make_async_copy(src, dst, load_sem.at[i])
        for i, (src, dst) in enumerate(
            (
                (feat_hbm, feat), (w1_hbm, w1), (coords_hbm, coords),
                (tiles_hbm, tiles.at[pl.ds(0, SLOTS)]), (b1_hbm, b1), (w2_hbm, w2), (b2_hbm, b2),
            )
        )
    ]
    for load in loads:
        load.start()

    loads[0].wait()
    loads[1].wait()
    zb[0, core, 0, 0] = jnp.dot(
        feat[...], w1[...], precision=lax.Precision.HIGHEST, preferred_element_type=jnp.float32
    ).astype(jnp.bfloat16)

    pl.semaphore_wait(barrier, len(peers))

    def z_copy(layer, i):
        d = SEND_Z[i]
        return remote(
            zb.at[layer, core, 0, 0], zb.at[layer, core, rank[-d], 0],
            z_send.at[layer, i], z_recv.at[layer, rank[-d]], at(0, d, core),
        )

    def x_copy(layer, dz, i):
        d, k = FAR_X[i], rank[dz]
        return remote(
            zb.at[layer, core, k, 0], zb.at[layer, core, k, -d % NX],
            x_send.at[layer, k, i], x_recv.at[layer, k], at(d, 0, core),
        )

    def pass_x_on(layer, i):
        d = NEAR_Z[i]
        return remote(
            zb.at[layer, core, 0, pl.ds(1, NX - 1)], zb.at[layer, core, rank[-d], pl.ds(1, NX - 1)],
            zx_send.at[layer, i], x_recv.at[layer, rank[-d]], at(0, d, core),
        )

    def c_copy(layer, b):
        first, size = rank[BUNDLES[b][0]], len(BUNDLES[b])
        block = zb.at[layer, core, pl.ds(first, size)]
        return remote(block, block, c_send.at[layer, b], c_recv.at[layer, b], sibling)

    def arrived(block, recv):
        remote(block, block, z_send.at[0, 0], recv, sibling).wait_recv()

    def multiply(layer, dz):
        za = (z + dz + NZ) % NZ
        places = [((x + dx) % NX) * NZ + za for dx in range(NX)]
        k = rank[dz]
        rhs = jnp.concatenate([zb[layer, c, k, dx] for dx in range(NX) for c in range(2)], axis=0)
        for r in range(RT):
            lhs = jnp.concatenate(
                [tiles[table[0, r * NX * NZ + p]] for p in places], axis=1
            )
            acc[layer, 2 * r : 2 * r + 2] += jnp.dot(
                lhs, rhs, preferred_element_type=jnp.float32
            ).reshape(2, NODE, TILE)

    def start_gather(layer):
        for i in range(len(FAR_X)):
            x_copy(layer, 0, i).start()
        for i in range(len(SEND_Z)):
            z_copy(layer, i).start()
        acc[layer] = jnp.zeros((NY, NODE, TILE), jnp.float32)

    def take_z(layer, dz):
        k = rank[dz]
        arrived(zb.at[layer, core, k, 0], z_recv.at[layer, k])
        if dz not in NEAR_Z:
            for i in range(len(FAR_X)):
                x_copy(layer, dz, i).start()

    def take_x(layer, dz):
        arrived(zb.at[layer, core, rank[dz], pl.ds(1, NX - 1)], x_recv.at[layer, rank[dz]])
        if dz == 0:
            for i in range(2):
                pass_x_on(layer, i).start()

    def gather_multiply(layer):
        for dz in BY_Z[: opt["ZCOUNT"]]:
            take_z(layer, dz)
        take_x(layer, 0)
        for dz in BY_Z[opt["ZCOUNT"] :] + NEAR_Z:
            take_z(layer, dz)
        for t in range(len(BUNDLES) + LAG):
            if t < len(BUNDLES):
                for dz in BUNDLES[t]:
                    if dz != 0:
                        take_x(layer, dz)
                c_copy(layer, t).start()
            if t >= LAG:
                b = t - LAG
                first, size = rank[BUNDLES[b][0]], len(BUNDLES[b])
                arrived(zb.at[layer, 1 - core, pl.ds(first, size)], c_recv.at[layer, b])
                for dz in BUNDLES[b]:
                    multiply(layer, dz)

    def drain(layer):
        for i in range(len(SEND_Z)):
            z_copy(layer, i).wait_send()
        for i in range(2):
            pass_x_on(layer, i).wait_send()
        for dz in order:
            for i in range(len(FAR_X) if dz not in NEAR_Z else 0):
                x_copy(layer, dz, i).wait_send()
        for b in range(len(BUNDLES)):
            c_copy(layer, b).wait_send()

    def wide_copy(layer, i):
        d = WIDE_Y[i]
        return remote(
            acc.at[layer, (col + d + NY) % NY], wide.at[layer, WIDE_Y.index(-d)],
            r1_send.at[layer, i], r1_recv.at[layer, 0], at(0, 0, core, d),
        )

    def narrow_copy(layer, i):
        d = NARROW_Y[i]
        return remote(
            narrow.at[layer, 0, i], narrow.at[layer, 1, NARROW_Y.index(-d if d != 4 else 4)],
            r1_send.at[layer, len(WIDE_Y) + i], r1_recv.at[layer, 1], at(0, 0, core, d),
        )

    start_gather(0)
    loads[2].wait()
    lane = lax.broadcasted_iota(jnp.int32, (SLOTS, SLOTS), 1)
    slot = lax.broadcasted_iota(jnp.int32, (SLOTS, SLOTS), 0)
    place = coords[0:1, :] * (NX * NZ) + coords[1:2, :]
    place = jnp.where(lane[0:1] < count_ref[0, 0], place, -1)
    place = jnp.max(jnp.where(lane == slot, place, -1), axis=1, keepdims=True)
    hit = place == lax.broadcasted_iota(jnp.int32, (SLOTS, 2 * TILE), 1)
    used = jnp.where(hit, lax.broadcasted_iota(jnp.int32, (SLOTS, 2 * TILE), 0), SLOTS)
    table_v[...] = jnp.min(used, axis=0, keepdims=True)
    to_table = pltpu.make_async_copy(table_v, table, table_sem)
    to_table.start()
    tiles[SLOTS] = jnp.zeros((TILE, TILE), jnp.bfloat16)
    for load in loads[3:]:
        load.wait()
    to_table.wait()

    for layer in range(nl - 1):
        gather_multiply(layer)
        for i, d in enumerate(NARROW_Y):
            narrow[layer, 0, i] = acc[layer, (col + d + NY) % NY].astype(jnp.bfloat16)
            narrow_copy(layer, i).start()
        for i in range(len(WIDE_Y)):
            wide_copy(layer, i).start()
        total = acc[layer, col] + b1[...]
        if WIDE_Y:
            arrived(wide.at[layer], r1_recv.at[layer, 0])
            total += jnp.sum(wide[layer], axis=0)
        arrived(narrow.at[layer, 1], r1_recv.at[layer, 1])
        total += jnp.sum(narrow[layer, 1].astype(jnp.float32), axis=0)
        hidden = jnp.maximum(total, 0.0)
        zb[layer + 1, core, 0, 0] = jnp.dot(
            hidden, w2[...], precision=lax.Precision.HIGHEST, preferred_element_type=jnp.float32
        ).astype(jnp.bfloat16)
        start_gather(layer + 1)

    last = nl - 1
    gather_multiply(last)
    part2[...] = acc[last].astype(jnp.bfloat16)
    FAR_Y = (4, 3, -3, 2, -2, 1, -1)

    def r2_copy(i):
        d = FAR_Y[i]
        return remote(
            part2.at[(col + d + NY) % NY], back2.at[-d % NY - 1], r2_send.at[i], r2_recv, at(0, 0, core, d)
        )

    for i in range(len(FAR_Y)):
        r2_copy(i).start()

    for layer in range(nl - 1):
        for i in range(len(WIDE_Y)):
            wide_copy(layer, i).wait_send()
        for i in range(len(NARROW_Y)):
            narrow_copy(layer, i).wait_send()
    for layer in range(nl):
        drain(layer)

    own = acc[last, col] + b2[...]
    arrived(back2, r2_recv)
    out_ref[...] = own + jnp.sum(back2[...].astype(jnp.float32), axis=0)
    for i in range(len(FAR_Y)):
        r2_copy(i).wait_send()


def on_device(
    features, tile_coords, tile_count, tile_values, w_first, bias_first, w_second, bias_second, opt=OPT, cid=0, name=None
):
    hbm = pl.BlockSpec(memory_space=pltpu.HBM)
    dma = pltpu.SemaphoreType.DMA
    bf16, f32, i32 = jnp.bfloat16, jnp.float32, jnp.int32
    nl, nw, nn = opt["nl"], len(opt["WIDE_Y"]), len(opt["NARROW_Y"])
    in_hbm = (
        tile_coords[0, 0].T, features, tile_values[0, 0],
        w_first, bias_first.reshape(1, TILE), w_second, bias_second.reshape(1, TILE),
    )
    return pl.pallas_call(
        functools.partial(kernel, opt),
        name=name,
        out_shape=jax.ShapeDtypeStruct((NODE, TILE), f32),
        in_specs=[pl.BlockSpec(memory_space=pltpu.SMEM)] + [hbm] * 7,
        out_specs=pl.BlockSpec(memory_space=pltpu.VMEM),
        scratch_shapes=[
            pltpu.VMEM((2, SLOTS), i32),
            pltpu.VMEM((NODE, TILE), f32),
            pltpu.VMEM((SLOTS + 1, TILE, TILE), bf16),
            pltpu.VMEM((TILE, TILE), f32),
            pltpu.VMEM((1, TILE), f32),
            pltpu.VMEM((TILE, TILE), f32),
            pltpu.VMEM((1, TILE), f32),
            pltpu.VMEM((1, 2 * TILE), i32),
            pltpu.SMEM((1, 2 * TILE), i32),
            pltpu.VMEM((nl, 2, NZ, NX, NODE, TILE), bf16),
            pltpu.VMEM((nl, NY, NODE, TILE), f32),
            pltpu.VMEM((nl - 1, max(nw, 1), NODE, TILE), f32),
            pltpu.VMEM((nl - 1, 2, nn, NODE, TILE), bf16),
            pltpu.VMEM((NY, NODE, TILE), bf16),
            pltpu.VMEM((NY - 1, NODE, TILE), bf16),
            dma((7,)), dma,
            dma((nl, 11)), dma((nl, NZ)), dma((nl, 2)), dma((nl, NZ, 3)), dma((nl, NZ)), dma((nl, NZ)), dma((nl, NZ)),
            dma((nl - 1, 7)), dma((nl - 1, 2)), dma((7,)), dma,
        ],
        compiler_params=pltpu.CompilerParams(
            collective_id=cid, has_side_effects=True, vmem_limit_bytes=48 * 2**20
        ),
        cost_estimate=pl.CostEstimate(flops=3 * 10**9, bytes_accessed=2 * 10**6, transcendentals=0),
    )(tile_count, *[pltpu.with_memory_space_constraint(a, pltpu.HBM) for a in in_hbm])


def solution(mesh):
    return jax.shard_map(
        on_device,
        mesh=mesh,
        in_specs=(
            P(("row", "col"), None),
            P("row", "col", None, None),
            P("row", "col"),
            P("row", "col", None, None, None),
            P(),
            P(),
            P(),
            P(),
        ),
        out_specs=P(("row", "col"), None),
        check_vma=False,
    )
```

time: 68.5 us -> 63.4 us (0.926)
  Pallas kernels: 67.1 us -> 61.9 us
    pallas_call x1, Pallas kernels: 67.1 us -> 61.9 us  [on_device(): pl.pallas_call(functools.partial(kernel, opt), name=name, out_shape=jax.S...]
where the time goes in v4:
time: 63.4 us; the launch traced here: 63.2 us
  Pallas kernels  61.9 us (98%)
  between operations  0.66 us (1%)
    pallas_call x1, Pallas kernels, on_device(): pl.pallas_call(functools.partial(kernel, opt), name=name, out_shape=jax.S...  61.9 us

profile of v4, /device:TPU:1, one launch (start us, length us, event | category | flops | bytes accessed | tf_op | source)
XLA Modules:
  0.0 63.2 jit_solution(381769223838597784)
XLA Ops:
  0.7 61.9 %shard_map.82 = f32[64,128]{1,0:T(8,128)S(1)} custom-call(s32[1,1]{1,0:T(1,128)S(6)} %copy.10.count_ref, s32[2,54]{1,0:T(2,128)} %bitcast.7, f32[64,128]{1,0:T(8,128)} %feat_hbm.1, bf16[54,128,128]{2,1,0:T(8,128)(2,1)} %bitcast.6, f32[128,128]{1,0:T(8,128)} %w1_hbm.1, f32[1,128]{1,0:T(1,128)} %bitcast.8, f32[128,128]{1,0:T(8,128)} %w2_hbm.1, f32[1,128]{1,0:T(1,128)} %bitcast.9), custom_call_target="tpu_custom_call" | custom-call | flops 3000000000 | bytes 2000000 | tf_op jit(solution)/shard_map/pallas_call | solution.py:265
  62.6 0.6 copy.11

commit v5 on v4

--- a/solution.py
+++ b/solution.py
@@ -186,6 +186,13 @@
             r1_send.at[layer, len(WIDE_Y) + i], r1_recv.at[layer, 1], at(0, 0, core, d),
         )
 
+    def settle(layer):
+        for i in range(len(WIDE_Y)):
+            wide_copy(layer, i).wait_send()
+        for i in range(len(NARROW_Y)):
+            narrow_copy(layer, i).wait_send()
+        drain(layer)
+
     start_gather(0)
     loads[2].wait()
     lane = lax.broadcasted_iota(jnp.int32, (SLOTS, SLOTS), 1)
@@ -221,6 +228,7 @@
             hidden, w2[...], precision=lax.Precision.HIGHEST, preferred_element_type=jnp.float32
         ).astype(jnp.bfloat16)
         start_gather(layer + 1)
+        settle(layer)
 
     last = nl - 1
     gather_multiply(last)
@@ -236,13 +244,7 @@
     for i in range(len(FAR_Y)):
         r2_copy(i).start()
 
-    for layer in range(nl - 1):
-        for i in range(len(WIDE_Y)):
-            wide_copy(layer, i).wait_send()
-        for i in range(len(NARROW_Y)):
-            narrow_copy(layer, i).wait_send()
-    for layer in range(nl):
-        drain(layer)
+    drain(last)
 
     own = acc[last, col] + b2[...]
     arrived(back2, r2_recv)

time: 63.4 us -> 63.4 us (level)
  no operation moved by 1% of the time
where the time goes in v5:
time: 63.4 us; the launch traced here: 63.2 us
  Pallas kernels  61.9 us (98%)
  between operations  0.66 us (1%)
    pallas_call x1, Pallas kernels, on_device(): pl.pallas_call(functools.partial(kernel, opt), name=name, out_shape=jax.S...  61.9 us

profile of v5, /device:TPU:1, one launch (start us, length us, event | category | flops | bytes accessed | tf_op | source)
XLA Modules:
  0.0 63.2 jit_solution(13654512547015943454)
XLA Ops:
  0.7 61.9 %shard_map.82 = f32[64,128]{1,0:T(8,128)S(1)} custom-call(s32[1,1]{1,0:T(1,128)S(6)} %copy.10.count_ref, s32[2,54]{1,0:T(2,128)} %bitcast.7, f32[64,128]{1,0:T(8,128)} %feat_hbm.1, bf16[54,128,128]{2,1,0:T(8,128)(2,1)} %bitcast.6, f32[128,128]{1,0:T(8,128)} %w1_hbm.1, f32[1,128]{1,0:T(1,128)} %bitcast.8, f32[128,128]{1,0:T(8,128)} %w2_hbm.1, f32[1,128]{1,0:T(1,128)} %bitcast.9), custom_call_target="tpu_custom_call" | custom-call | flops 3000000000 | bytes 2000000 | tf_op jit(solution)/shard_map/pallas_call | solution.py:267
  62.6 0.6 copy.11
